TPU v7x, 32 devices: a whole 2x2x4 slice. The times are simulated.
32 devices in a mesh: cx: 8 (over y, x, core), tp: 4 (over z).
Axes of the slice: x: 2, y: 2, z: 4, core: 2. Of those that a mesh axis runs over, the one named last changes fastest.
Arguments:
- layer_input: bfloat16 [1024, 3072], P('cx', 'tp'), may hold values from -40 to 40
- queries: bfloat16 [1024, 4096], P('cx', 'tp'), may hold values from -6 to 6
- keys: bfloat16 [1024, 4096], P('cx', 'tp'), may hold values from -6 to 6
- values: bfloat16 [1024, 4096], P('cx', 'tp'), may hold values from -6 to 6
- gate_input: bfloat16 [1024, 4096], P('cx', 'tp'), may hold values from -6 to 6
- log_decay: float32 [32, 1024], P('tp', 'cx'), may hold values from -1 to 0
- prior_state: float32 [32, 128, 128], P('tp'), may hold values from -192 to 192
- attn_gain: float32 [4096], P('tp'), may hold values from 0.5 to 1.5
- out_weight: bfloat16 [4096, 3072], P('tp'), may hold values from -0.09375 to 0.09375
- moe_gain: float32 [3072], replicated, may hold values from 0.5 to 1.5
- router: bfloat16 [3072, 4], replicated, may hold values from -0.109375 to 0.109375
- expert_ids: int32 [1024, 2], P('cx'), may hold values from 0 to 3, all different within a row; in each aligned block of 128 rows (0 to 127, 128 to 255, ...) at most 128 rows name the same one
- w_gate: bfloat16 [8, 3072, 3072], P('cx', None, 'tp'), may hold values from -0.109375 to 0.109375
- w_up: bfloat16 [8, 3072, 3072], P('cx', None, 'tp'), may hold values from -0.109375 to 0.109375
- w_down: bfloat16 [8, 3072, 3072], P('cx', 'tp'), may hold values from -0.078125 to 0.078125
Outputs:
- mixed: bfloat16 [1024, 3072], P('cx', 'tp')
Inputs may be any that keep to these rules, and one draw needn't show every extreme that they name: `expert_ids`: each row names 2 different experts. Among the rows of one index of cx no expert is named by more than 128 rows, and in every draw some expert is named by exactly 128 of them.
All inputs are finite; a program needn't handle non-finite values.
Results may differ from a plain program's by a relative error of at most 0.0085.
Values may be sent and summed in bfloat16 or wider, within the bound.
A program may use at most 128 MiB of HBM per device.

v0:
```python
import jax
import jax.numpy as jnp
from jax import lax
from jax.sharding import PartitionSpec as P

epsilon = 1e-06
highest_precision = lax.Precision.HIGHEST


def prefix(shard, axis, combine, identity):
    peers, index = (lax.axis_size(axis), lax.axis_index(axis))
    everything = jax.tree.map(lambda part: lax.all_gather(part, axis), shard)
    start = jax.tree.map(
        lambda part, zero: jnp.broadcast_to(jnp.asarray(zero, part.dtype), part.shape),
        shard,
        identity,
    )

    def lap(k, before):
        reached = k < index
        new = combine(before, jax.tree.map(lambda part: part[k], everything))
        return jax.tree.map(lambda a, b: jnp.where(reached, a, b), new, before)

    return lax.fori_loop(0, peers, lap, start)


def feed_forward(routed, gate_weight, up_weight, down_weight):
    gated = jnp.dot(routed, gate_weight, preferred_element_type=jnp.float32)
    lifted = jnp.dot(routed, up_weight, preferred_element_type=jnp.float32)
    activated = (jax.nn.silu(gated) * lifted).astype(jnp.bfloat16)
    return jnp.dot(activated, down_weight, preferred_element_type=jnp.float32)


def combine_states(earlier, later):
    return (earlier[0] + later[0], jnp.exp(later[0])[:, None, None] * earlier[1] + later[1])


def shards(
    layer_input,
    queries,
    keys,
    values,
    gate_input,
    log_decay,
    prior_state,
    attn_gain,
    out_weight,
    moe_gain,
    router,
    expert_ids,
    w_gate,
    w_up,
    w_down,
):
    positions = queries.shape[0]
    heads_here = log_decay.shape[0]
    head_size = prior_state.shape[1]
    query_vectors = queries.reshape(positions, heads_here, head_size)
    key_rows = keys.reshape(positions, heads_here, head_size)
    value_single_float = values.reshape(positions, heads_here, head_size).astype(jnp.float32)
    running_state = jnp.cumsum(log_decay, axis=1)
    causal = (jnp.arange(positions)[:, None] >= jnp.arange(positions)[None, :])[None]
    spread = running_state[:, :, None] - running_state[:, None, :]
    weights = jnp.where(causal, jnp.exp(jnp.where(causal, spread, 0.0)), 0.0)
    scores = (
        jnp.einsum("thk,shk->hts", query_vectors, key_rows, preferred_element_type=jnp.float32)
        * weights
    )
    inner = jnp.einsum("hts,shv->thv", scores, value_single_float, precision=highest_precision)
    trailing_rows = jnp.exp(running_state[:, -1:] - running_state)
    key_single_float = key_rows.astype(jnp.float32) * trailing_rows.T[:, :, None]
    within_block_state = jnp.einsum(
        "gpc,gpw->pcw", key_single_float, value_single_float, precision=highest_precision
    )
    total_decay = running_state[:, -1]
    identity = (
        jnp.zeros((heads_here,), jnp.float32),
        jnp.zeros((heads_here, head_size, head_size), jnp.float32),
    )
    before_total, before_state = prefix(
        (total_decay, within_block_state), "cx", combine_states, identity
    )
    incoming_state = jnp.exp(before_total)[:, None, None] * prior_state + before_state
    carried_contribution = jnp.exp(running_state).T[:, :, None] * jnp.einsum(
        "rxg,xgd->rxd",
        query_vectors.astype(jnp.float32),
        incoming_state,
        precision=highest_precision,
    )
    attended = inner + carried_contribution
    squares = jnp.mean(attended * attended, axis=-1, keepdims=True)
    gating = jax.nn.sigmoid(
        gate_input.astype(jnp.float32).reshape(positions, heads_here, head_size)
    )
    normed = (
        attended * lax.rsqrt(squares + epsilon) * attn_gain.reshape(heads_here, head_size) * gating
    )
    normed = normed.astype(jnp.bfloat16).reshape(positions, heads_here * head_size)
    partial_rows = jnp.dot(normed, out_weight, preferred_element_type=jnp.float32)
    model_width = out_weight.shape[1]
    width_share = layer_input.shape[1]
    column_start = lax.axis_index("tp") * width_share
    own_columns = lax.dynamic_slice_in_dim(
        partial_rows, column_start, width_share, 1
    ) + layer_input.astype(jnp.float32)
    partial_rows = lax.dynamic_update_slice_in_dim(partial_rows, own_columns, column_start, 1)
    expert_count = router.shape[1]
    hidden_state = lax.psum(partial_rows, "tp")
    row_mean = jnp.mean(hidden_state * hidden_state, axis=-1, keepdims=True)
    full_input = (hidden_state * lax.rsqrt(row_mean + epsilon) * moe_gain).astype(jnp.bfloat16)
    logits = jnp.dot(full_input, router, preferred_element_type=jnp.float32)
    hidden_share = lax.dynamic_slice_in_dim(hidden_state, column_start, width_share, 1)
    matched = expert_ids[:, :, None] == jnp.arange(expert_count, dtype=jnp.int32)[None, None, :]
    chosen = jnp.sum(jnp.where(matched, logits[:, None, :], 0.0), axis=-1)
    margin = chosen[:, 0] - chosen[:, 1]
    mixing = jnp.stack([jax.nn.sigmoid(margin), jax.nn.sigmoid(-margin)], axis=1)
    choices_made = expert_ids.shape[1]
    onehot = matched.reshape(positions * choices_made, expert_count).astype(jnp.int32)
    before = jnp.cumsum(onehot, axis=0) - onehot
    position = jnp.sum(before * onehot, axis=1).reshape(positions, choices_made)
    capacity = 8 * positions // lax.axis_size("cx")
    at_slot = position[:, :, None] == jnp.arange(capacity, dtype=jnp.int32)[None, None, :]
    picked = matched[:, :, :, None] & at_slot[:, :, None, :]
    dispatch = (
        jnp.sum(picked, axis=1).astype(jnp.bfloat16).reshape(positions, expert_count * capacity)
    )
    weighting = jnp.sum(jnp.where(picked, mixing[:, :, None, None], 0.0), axis=1).reshape(
        positions, expert_count * capacity
    )
    gate_weight = w_gate[0]
    up_weight = w_up[0]
    down_weight = w_down[0]
    outgoing = jnp.einsum(
        "tm,td->md", dispatch, full_input, preferred_element_type=jnp.float32
    ).astype(jnp.bfloat16)
    outgoing = jnp.repeat(outgoing.reshape(expert_count, capacity, model_width), 2, axis=0)
    received = lax.all_to_all(outgoing, "cx", split_axis=0, concat_axis=0, tiled=True)
    owners, slots, columns = received.shape
    produced = feed_forward(
        received.reshape(owners * slots, columns), gate_weight, up_weight, down_weight
    )
    returned = lax.all_to_all(
        produced.reshape(owners, slots, columns).astype(jnp.bfloat16),
        "cx",
        split_axis=0,
        concat_axis=0,
        tiled=True,
    ).astype(jnp.float32)
    halves = jnp.sum(returned.reshape(expert_count, 2, capacity, model_width), axis=1)
    moe_rows = jnp.dot(
        weighting,
        halves.reshape(expert_count * capacity, model_width),
        precision=highest_precision,
        preferred_element_type=jnp.float32,
    )
    moe_share = lax.psum_scatter(
        moe_rows.astype(jnp.bfloat16), "tp", scatter_dimension=1, tiled=True
    ).astype(jnp.float32)
    return (hidden_share + moe_share).astype(jnp.bfloat16)


def solution(mesh):
    placed = (
        P("cx", "tp"),
        P("cx", "tp"),
        P("cx", "tp"),
        P("cx", "tp"),
        P("cx", "tp"),
        P("tp", "cx"),
        P("tp", None, None),
        P("tp"),
        P("tp", None),
        P(),
        P(),
        P("cx", None),
        P("cx", None, "tp"),
        P("cx", None, "tp"),
        P("cx", "tp", None),
    )
    return jax.shard_map(
        shards, mesh=mesh, in_specs=placed, out_specs=P("cx", "tp"), check_vma=False
    )
```

profile of v0, /device:TPU:0, one launch (start us, length us, event | category | flops | bytes accessed | tf_op | source)
XLA Modules:
  0.0 348.2 jit_solution(2357637244699221982)
XLA Ops:
  6.5 1.0 reduce_window_sum.26
  7.6 0.2 slice_reduce_fusion
  7.8 0.1 exponential_bitcast_fusion.1
  7.8 1.1 copy.81
  9.0 1.2 fusion.15
  10.2 0.0 all-gather.4.cloned.1.call-update
  10.2 0.0 all-reduce.3.cloned.1.call-start
  10.3 1.2 dynamic-slice
  12.2 0.2 dynamic-update-slice
  12.4 15.3 %all-reduce = f32[64]{0:T(128)S(1)} all-reduce(f32[64]{0:T(128)S(1)} %dynamic-update-slice), channel_id=2, replica_groups=mesh['cx'=8,'tp'=4] {'cx'}, use_global_device_ids=true, to_apply=%add | all-reduce | flops 64 | bytes 512
  27.7 0.1 reshape.121
  27.8 1.1 add_divide_fusion
  28.9 0.2 copy.73
  29.1 0.2 convolution_multiply_fusion
  29.4 20.4 %all-gather.4.cloned.1.call-done = f32[64,128,128]{2,1,0:T(8,128)} async-done(((f32[8,128,128]{2,1,0:T(8,128)}), f32[64,128,128]{2,1,0:T(8,128)}) %all-gather.4.cloned.1.call-update) | async-done | bytes 4194320 | tf_op jit(solution)/shard_map/all_gather | solution.py:12
  49.8 9.8 %while.16 = (s32[]{:T(128)}, f32[8]{0:T(128)S(1)}, f32[8,128,128]{2,1,0:T(8,128)S(1)}, s32[]{:T(128)}, f32[8,8]{1,0:T(8,128)S(1)}, /*index=5*/f32[8,8,128,128]{3,2,1,0:T(8,128)}, s32[]{:T(128)}, s32[]{:T(128)}) while((s32[]{:T(128)}, f32[8]{0:T(128)S(1)}, f32[8,128,128]{2,1,0:T(8,128)S(1)}, s32[]{:T(128)}, f32[8,8]{1,0:T(8,128)S(1)}, ...), condition=%wide.region_2.3_spmd.clone, body=%wide.region_1.2_spmd.clone.sunk | while | flops 524316 | bytes 1573139 | solution.py:24
  49.8 1.2 fusion.49
  51.1 1.2 fusion.49
  52.3 1.2 fusion.49
  53.5 1.2 fusion.49
  54.8 1.2 fusion.49
  56.0 1.2 fusion.49
  57.2 1.2 fusion.49
  58.4 1.2 fusion.49
  59.6 0.7 fusion.10
  60.3 0.7 multiply_reduce_fusion.1
  61.1 0.2 multiply_convert_fusion.2
  61.3 3.8 %fusion.32 = f32[128,3072]{1,0:T(8,128)S(1)} fusion(bf16[128,1024]{0,1:T(8,128)(2,1)S(1)} %bitcast.114, bf16[1024,3072]{1,0:T(8,128)(2,1)} %param.25), kind=kOutput, calls=%fused_computation.69 | convolution fusion | flops 805306368 | bytes 8126464 | tf_op jit(solution)/shard_map/dot_general | solution.py:99
  65.1 0.1 add_dynamic-update-slice_fusion
  65.2 1.1 copy-done.3
  66.4 0.0 all-reduce.3.cloned.1.call-update
  66.4 0.1 copy.74
  66.5 0.1 eq.62
  66.7 0.1 eq.58
  66.8 1.2 reduce-window.6
  68.0 0.1 slice.21
  68.1 0.1 copy.76
  68.3 0.1 copy.77
  68.4 0.1 add_bitcast_fusion
  68.5 0.1 eq.66
  68.6 0.1 copy.78
  68.7 0.1 iota_compare_fusion
  68.8 0.2 fusion.12
  69.0 0.1 copy.79
  69.2 66.5 %all-reduce.3.cloned.1.call-done = f32[128,3072]{1,0:T(8,128)} async-done(((f32[128,3072]{1,0:T(8,128)}), f32[128,3072]{1,0:T(8,128)}) %all-reduce.3.cloned.1.call-update) | async-done | bytes 1572880 | tf_op jit(solution)/shard_map/psum | solution.py:108
  135.7 1.6 multiply_reduce_fusion
  137.3 2.5 convolution_convert_fusion.1
  139.8 0.0 slice-start
  139.8 0.8 broadcast_in_dim.73
  140.6 75.3 %all_to_all.10 = bf16[8,128,3072]{2,1,0:T(8,128)(2,1)S(1)} all-to-all(bf16[8,128,3072]{2,1,0:T(8,128)(2,1)S(1)} %bitcast.109), channel_id=1, replica_groups=mesh['cx'=8,'tp'=4] {'cx'}, dimensions={0} | all-to-all | bytes 12582912 | tf_op jit(solution)/shard_map/all_to_all | solution.py:137
  215.9 5.1 %fusion.2 = f32[1024,768]{1,0:T(8,128)S(1)} fusion(bf16[1024,3072]{1,0:T(8,128)(2,1)S(1)} %bitcast.111, bf16[1,3072,768]{2,1,0:T(8,128)(2,1)S(1)} %bitcast.122), kind=kOutput, calls=%fused_computation.9 | convolution fusion | flops 4831838208 | bytes 14155776 | tf_op jit(solution)/shard_map/dot_general | solution.py:29
  221.0 0.0 slice-start.5
  221.0 5.4 %multiply_convert_fusion = bf16[1024,768]{1,0:T(8,128)(2,1)S(1)} fusion(f32[1024,768]{1,0:T(8,128)S(1)} %fusion.2, bf16[1024,3072]{1,0:T(8,128)(2,1)S(1)} %bitcast.112, bf16[1,3072,768]{2,1,0:T(8,128)(2,1)S(1)} %bitcast.124), kind=kOutput, calls=%fused_computation.16 | convolution fusion | flops 4836556800 | bytes 15728640 | tf_op jit(solution)/shard_map/dot_general | solution.py:28
  226.4 7.1 %convolution_convert_fusion = bf16[8,128,3072]{2,1,0:T(8,128)(2,1)} fusion(bf16[8,128,768]{2,1,0:T(8,128)(2,1)S(1)} %bitcast.127, bf16[1,768,3072]{2,1,0:T(8,128)(2,1)S(1)} %bitcast.126), kind=kOutput, calls=%fused_computation.7 | convolution fusion | flops 4834983936 | bytes 12582912 | tf_op jit(solution)/shard_map/dot_general | solution.py:31
  233.5 4.9 %all-to-all-start.1 = ((bf16[8,128,3072]{2,1,0:T(8,128)(2,1)}), bf16[8,128,3072]{2,1,0:T(8,128)(2,1)}, u32[]{:S(2)}, u32[]{:S(2)}) async-start(bf16[8,128,3072]{2,1,0:T(8,128)(2,1)} %convolution_convert_fusion), calls=%async_computation.1 | async-start | bytes 12582912 | tf_op jit(solution)/shard_map/all_to_all | solution.py:142
  238.3 0.3 reduce-scatter.2.cloned.1.call-start
  238.6 0.4 fusion.31
  239.1 0.2 fusion.11
  239.3 70.6 %all-to-all-done.1 = bf16[8,128,3072]{2,1,0:T(8,128)(2,1)} async-done(((bf16[8,128,3072]{2,1,0:T(8,128)(2,1)}), bf16[8,128,3072]{2,1,0:T(8,128)(2,1)}, u32[]{:S(2)}, u32[]{:S(2)}) %all-to-all-start.1) | async-done | bytes 6291488 | tf_op jit(solution)/shard_map/all_to_all | solution.py:142
  309.9 5.1 %convert_reduce_fusion = f32[4,128,3072]{2,1,0:T(8,128)S(1)} fusion(bf16[8,128,3072]{2,1,0:T(8,128)(2,1)} %all-to-all-done.1), kind=kLoop, calls=%fused_computation.6 | loop fusion | flops 4718592 | bytes 12582912 | tf_op jit(solution)/shard_map/reduce_sum | solution.py:149
  315.0 4.3 %fusion.6 = bf16[128,3072]{1,0:T(8,128)(2,1)} fusion(f32[128,4,128]{2,0,1:T(8,128)S(1)} %fusion.11, f32[4,128,3072]{2,1,0:T(8,128)S(1)} %convert_reduce_fusion), kind=kOutput, calls=%fused_computation.15 | convolution fusion | flops 2416312320 | bytes 7340032 | tf_op jit(solution)/shard_map/dot_general | solution.py:150
  319.3 0.0 reduce-scatter.2.cloned.1.call-update
  319.3 20.7 %reduce-scatter.2.cloned.1.call-done = bf16[128,768]{1,0:T(8,128)(2,1)} async-done(((bf16[128,3072]{1,0:T(8,128)(2,1)}), bf16[128,768]{1,0:T(8,128)(2,1)}) %reduce-scatter.2.cloned.1.call-update) | async-done | bytes 196624 | tf_op jit(solution)/shard_map/reduce_scatter | solution.py:156
  340.1 1.6 add_convert_fusion
  (59 shorter events, 0.4 us)
Async XLA Ops:
  6.5 2.4 copy-start
  6.5 22.6 %copy-start.5 = (bf16[128,1024]{1,0:T(8,128)(2,1)S(1)}, bf16[128,1024]{1,0:T(8,128)(2,1)}, u32[]{:S(2)}) copy-start(bf16[128,1024]{1,0:T(8,128)(2,1)} %param.18) | copy-start | bytes 786436
  6.5 43.3 %all-gather.4.cloned.1.call-start = ((), (), s32[]{:S(2)}) async-start(), calls=%async_computation.5 | async-start | bytes 4718592 | tf_op jit(solution)/shard_map/all_gather | solution.py:12
  10.2 125.5 %all-reduce.3.cloned.1.call-start = ((), (), s32[]{:S(2)}) async-start(), calls=%async_computation.3 | async-start | bytes 3145728 | tf_op jit(solution)/shard_map/psum | solution.py:108
  49.8 9.8 %copy-start.4 = (f32[8,128,128]{2,1,0:T(8,128)S(1)}, f32[8,128,128]{2,1,0:T(8,128)}, u32[]{:S(2)}) copy-start(f32[8,128,128]{2,1,0:T(8,128)} %param.23) | copy-start | bytes 1572868
  59.6 1.4 copy-start.10
  61.3 3.9 %copy-start.6 = (bf16[128,768]{1,0:T(8,128)(2,1)S(1)}, bf16[128,768]{1,0:T(8,128)(2,1)}, u32[]{:S(2)}) copy-start(bf16[128,768]{1,0:T(8,128)(2,1)} %param.17) | copy-start | bytes 589828
  61.3 5.1 %copy-start.9 = (s32[128,2]{0,1:T(2,128)S(1)}, s32[128,2]{0,1:T(2,128)}, u32[]{:S(2)}) copy-start(s32[128,2]{0,1:T(2,128)} %param.28) | copy-start | bytes 3076
  65.1 72.1 %copy-start.7 = (f32[3072]{0:T(1024)S(1)}, f32[3072]{0:T(1024)}, u32[]{:S(2)}) copy-start(f32[3072]{0:T(1024)} %param.26) | copy-start | bytes 36868
  65.2 1.2 copy-start.3
  139.8 76.1 %slice-start = ((s8[4718592]{0:T(1024)(128)(4,1)}), s8[524288]{0:T(1024)(128)(4,1)S(1)}, s32[]{:S(2)}) async-start(s8[4718592]{0:T(1024)(128)(4,1)} %bitcast.121), calls=%async_computation.6 | async-start | bytes 1048576
  140.6 75.3 %slice-start.1 = ((s8[4718592]{0:T(1024)(128)(4,1)}), s8[4194304]{0:T(1024)(128)(4,1)S(1)}, s32[]{:S(2)}) async-start(s8[4718592]{0:T(1024)(128)(4,1)} %bitcast.121), calls=%async_computation.7 | async-start | bytes 8388608
  140.6 80.4 %slice-start.2 = ((s8[4718592]{0:T(1024)(128)(4,1)}), s8[4194304]{0:T(1024)(128)(4,1)S(1)}, s32[]{:S(2)}) async-start(s8[4718592]{0:T(1024)(128)(4,1)} %bitcast.123), calls=%async_computation.8 | async-start | bytes 8388608
  215.9 5.1 %slice-start.3 = ((s8[4718592]{0:T(1024)(128)(4,1)}), s8[524288]{0:T(1024)(128)(4,1)S(1)}, s32[]{:S(2)}) async-start(s8[4718592]{0:T(1024)(128)(4,1)} %bitcast.123), calls=%async_computation.9 | async-start | bytes 1048576
  215.9 10.5 %slice-start.4 = ((s8[4718592]{0:T(1024)(128)(4,1)}), s8[4194304]{0:T(1024)(128)(4,1)S(1)}, s32[]{:S(2)}) async-start(s8[4718592]{0:T(1024)(128)(4,1)} %bitcast.125), calls=%async_computation.10 | async-start | bytes 8388608
  221.0 5.4 %slice-start.5 = ((s8[4718592]{0:T(1024)(128)(4,1)}), s8[524288]{0:T(1024)(128)(4,1)S(1)}, s32[]{:S(2)}) async-start(s8[4718592]{0:T(1024)(128)(4,1)} %bitcast.125), calls=%async_computation.11 | async-start | bytes 1048576
  233.5 5.2 %copy-start.2 = (f32[128,3072]{1,0:T(8,128)S(1)}, f32[128,3072]{1,0:T(8,128)}, u32[]{:S(2)}) copy-start(f32[128,3072]{1,0:T(8,128)} %all-reduce.3.cloned.1.call-done) | copy-start | bytes 4718596
  233.5 5.2 %copy-start.8 = (bf16[3072,4]{0,1:T(4,128)(2,1)S(1)}, bf16[3072,4]{0,1:T(4,128)(2,1)}, u32[]{:S(2)}) copy-start(bf16[3072,4]{0,1:T(4,128)(2,1)} %param.27) | copy-start | bytes 73732
  233.5 76.5 %all-to-all-start.1 = ((bf16[8,128,3072]{2,1,0:T(8,128)(2,1)}), bf16[8,128,3072]{2,1,0:T(8,128)(2,1)}, u32[]{:S(2)}, u32[]{:S(2)}) async-start(bf16[8,128,3072]{2,1,0:T(8,128)(2,1)} %convolution_convert_fusion), calls=%async_computation.1 | async-start | bytes 12582912 | tf_op jit(solution)/shard_map/all_to_all | solution.py:142
  238.3 101.7 %reduce-scatter.2.cloned.1.call-start = ((), (), s32[]{:S(2)}) async-start(), calls=%async_computation.4 | async-start | bytes 983040 | tf_op jit(solution)/shard_map/reduce_scatter | solution.py:156
  309.9 31.8 %copy-start.1 = (bf16[128,1024]{1,0:T(8,128)(2,1)S(1)}, bf16[128,1024]{1,0:T(8,128)(2,1)}, u32[]{:S(2)}) copy-start(bf16[128,1024]{1,0:T(8,128)(2,1)} %param.20) | copy-start | bytes 786436
Sparse Core Ops, SparseCore 0:
  10.3 39.4 all-gather.3
  66.5 69.1 all-reduce.2
  319.4 20.5 reduce-scatter.1
where the time goes:
time: 349 us; the launch traced here: 348 us
  waiting for transfers between devices  178 us (51%)
  blocking collectives  90.6 us (26%)
  matrix products  31.2 us (9%)
  other arithmetic  22.4 us (6%)
  between operations  14.2 us (4%)
  local copies, waits for them, and re-layouts  6.11 us (2%)
  starting transfers between devices  5.18 us (1%)
    all_to_all x1, blocking collectives, shards(): lax.all_to_all(outgoing, 'cx', split_axis=0, concat_axis=0, tiled=True)  75.3 us
    all_to_all x1, waiting for transfers between devices, shards(): lax.all_to_all(produced.reshape(owners, slots, columns).astype(jnp.bfloat...  70.6 us
    psum x1, waiting for transfers between devices, shards(): hidden_state = lax.psum(partial_rows, 'tp')  66.5 us
    reduce_scatter x1, waiting for transfers between devices, shards(): lax.psum_scatter(moe_rows.astype(jnp.bfloat16), 'tp', scatter_dimension=1...  20.7 us
    all_gather x1, waiting for transfers between devices, prefix(): everything = jax.tree.map(lambda part: lax.all_gather(part, axis), shard)  20.4 us
    unnamed x1, blocking collectives  15.3 us
    select_n x8, other arithmetic, lap(): return jax.tree.map(lambda a, b: jnp.where(reached, a, b), new, before)  9.46 us
    dot_general x1, matrix products, feed_forward(): return jnp.dot(activated, down_weight, preferred_element_type=jnp.float32)  7.06 us
  transfers between devices with their start and end apart: 4, of which 4 were waited for; matrix products, arithmetic and copies ran while one was open for 2% of the time, Pallas kernels for 0%

commit v1 on v0

--- a/solution.py
+++ b/solution.py
@@ -1,6 +1,10 @@
+import functools
+
 import jax
 import jax.numpy as jnp
 from jax import lax
+from jax.experimental import pallas as pl
+from jax.experimental.pallas import tpu as pltpu
 from jax.sharding import PartitionSpec as P
 
 epsilon = 1e-06
@@ -35,7 +39,7 @@
     return (earlier[0] + later[0], jnp.exp(later[0])[:, None, None] * earlier[1] + later[1])
 
 
-def shards(
+def shards_routed(
     layer_input,
     queries,
     keys,
@@ -159,6 +163,545 @@
     return (hidden_share + moe_share).astype(jnp.bfloat16)
 
 
+MESH = pl.DeviceIdType.MESH
+VMEM_BYTES = 46 * 1024 * 1024
+CHIPS = 4
+PIECES = 4
+
+
+def neighbours():
+    cx, tp = lax.axis_index("cx"), lax.axis_index("tp")
+    sibling = cx + 1 - 2 * (cx % 2)
+    along_x = cx + 2 - 4 * ((cx // 2) % 2)
+    along_y = (cx + 4) % 8
+    return cx, tp, sibling, along_x, along_y
+
+
+def partners(tp):
+    return [tp, tp + 1 - 2 * (tp % 2), (tp + 2) % 4, 3 - tp]
+
+
+def greet(devices):
+    barrier = pltpu.get_barrier_semaphore()
+    for device in devices:
+        pl.semaphore_signal(barrier, inc=1, device_id=device, device_id_type=MESH)
+    pl.semaphore_wait(barrier, len(devices))
+
+
+class Copies:
+    def __init__(self, send, recv):
+        self.send, self.recv, self.numbers, self.started = send, recv, {}, []
+
+    def make(self, name, source, target, device):
+        number = self.numbers.setdefault(name, len(self.numbers))
+        return pltpu.make_async_remote_copy(
+            src_ref=source,
+            dst_ref=target,
+            send_sem=self.send.at[number],
+            recv_sem=self.recv.at[number],
+            device_id=device,
+            device_id_type=MESH,
+        )
+
+    def start(self, name, source, target, device):
+        copy = self.make(name, source, target, device)
+        copy.start()
+        self.started.append(copy)
+
+    def wait(self, name, landed, device):
+        self.make(name, landed, landed, device).wait_recv()
+
+    def drain(self):
+        for copy in self.started:
+            copy.wait_send()
+
+
+def plane_gather(copies, place, rows, split):
+    cx, tp, sibling, along_x, along_y = neighbours()
+    across = (along_x + 4) % 8
+    to_sibling, to_x, to_y = (sibling, tp), (along_x, tp), (along_y, tp)
+    parts = ((0, split), (split, rows - split))
+
+    def pair(owner):
+        return owner + 1 - 2 * (owner % 2)
+
+    def push(name, owner, piece, part, device):
+        ref = place(owner, piece, *part)
+        copies.start(name, ref, ref, device)
+
+    def arrive(name, owner, piece, part):
+        copies.wait(name, place(owner, piece, *part), to_sibling)
+
+    whole = (0, rows)
+
+    def stage(j, piece):
+        push(("x", j), cx, piece, whole, to_x)
+        push(("y", j), cx, piece, whole, to_y)
+        push(("own", j), cx, piece, whole, to_sibling)
+
+    def forward(j, piece):
+        arrive(("x", j), along_x, piece, whole)
+        push(("dy", j), along_x, piece, parts[0], to_y)
+        push(("sx", j), along_x, piece, whole, to_sibling)
+        arrive(("y", j), along_y, piece, whole)
+        push(("dx", j), along_y, piece, parts[1], to_x)
+        push(("sy", j), along_y, piece, whole, to_sibling)
+
+    def corner(j, piece):
+        arrive(("dy", j), across, piece, parts[0])
+        push(("sd0", j), across, piece, parts[0], to_sibling)
+        arrive(("dx", j), across, piece, parts[1])
+        push(("sd1", j), across, piece, parts[1], to_sibling)
+
+    def finish(j, piece, which):
+        if which == 0:
+            arrive(("own", j), pair(cx), piece, whole)
+        if which == 1:
+            arrive(("sx", j), pair(along_x), piece, whole)
+            arrive(("sy", j), pair(along_y), piece, whole)
+        if which == 2:
+            arrive(("sd0", j), pair(across), piece, parts[0])
+            arrive(("sd1", j), pair(across), piece, parts[1])
+
+    return stage, forward, corner, finish
+
+
+def state_kernel(rows, split, block_ref, all_ref, last_ref, send, recv, local):
+    cx, tp, sibling, along_x, along_y = neighbours()
+    own = pltpu.make_async_copy(block_ref, all_ref.at[cx], local)
+    own.start()
+    greet([(sibling, tp), (along_x, tp), (along_y, tp)])
+    own.wait()
+    copies = Copies(send, recv)
+
+    def place(owner, piece, first, count):
+        return all_ref.at[owner, pl.ds(first, count), :]
+
+    stage, forward, corner, finish = plane_gather(copies, place, rows, split)
+    stage(0, 0)
+    forward(0, 0)
+    corner(0, 0)
+    for which in range(3):
+        finish(0, 0, which)
+    last_ref[...] = all_ref[:, rows - 16 :, :].astype(jnp.float32)
+    copies.drain()
+
+
+def gather_states(block):
+    rows = block.shape[0]
+    return pl.pallas_call(
+        functools.partial(state_kernel, rows, rows // 32 * 16),
+        out_shape=(
+            jax.ShapeDtypeStruct((2 * CHIPS,) + block.shape, block.dtype),
+            jax.ShapeDtypeStruct((2 * CHIPS, 16, block.shape[1]), jnp.float32),
+        ),
+        in_specs=[pl.BlockSpec(memory_space=pltpu.VMEM)],
+        out_specs=(pl.BlockSpec(memory_space=pltpu.VMEM), pl.BlockSpec(memory_space=pltpu.VMEM)),
+        scratch_shapes=[
+            pltpu.SemaphoreType.DMA((9,)),
+            pltpu.SemaphoreType.DMA((9,)),
+            pltpu.SemaphoreType.DMA,
+        ],
+        compiler_params=pltpu.CompilerParams(
+            collective_id=1, has_side_effects=True, vmem_limit_bytes=VMEM_BYTES
+        ),
+        name="gather_states",
+    )(block)
+
+
+def layer_kernel(
+    partial_ref,
+    layer_ref,
+    gain_ref,
+    router_ref,
+    ids_ref,
+    gate_hbm,
+    up_hbm,
+    down_hbm,
+    out_ref,
+    hidden_ref,
+    all_ref,
+    squares,
+    gate_ref,
+    up_ref,
+    down_ref,
+    activated,
+    produced_ref,
+    paired,
+    outbox,
+    inbox,
+    corner_out,
+    x_out,
+    y_out,
+    corner_x,
+    corner_y,
+    x_in,
+    y_in,
+    z_out,
+    z_in,
+    send,
+    recv,
+    local,
+):
+    cx, tp, sibling, along_x, along_y = neighbours()
+    rows, share = layer_ref.shape
+    hidden_units = down_ref.shape[0]
+    width = down_ref.shape[1]
+    half = rows // 2
+    top, low = pl.ds(0, half), pl.ds(half, half)
+    peers = partners(tp)
+    across = (along_x + 4) % 8
+    to_sibling, to_x, to_y = (sibling, tp), (along_x, tp), (along_y, tp)
+    loads = [
+        pltpu.make_async_copy(source, target, local.at[k])
+        for k, (source, target) in enumerate(
+            ((gate_hbm, gate_ref), (up_hbm, up_ref), (down_hbm, down_ref))
+        )
+    ]
+    for load in loads:
+        load.start()
+    greet([to_sibling, to_x, to_y] + [(cx, peer) for peer in peers[1:]])
+    copies = Copies(send, recv)
+
+    def columns(piece):
+        return pl.ds(pl.multiple_of(piece * share, share), share)
+
+    outbox[3] = partial_ref[:, columns(peers[3])].astype(jnp.bfloat16)
+    copies.start(("sum", 3), outbox.at[3], inbox.at[2], (cx, peers[1]))
+    outbox[1] = partial_ref[:, columns(peers[1])].astype(jnp.bfloat16)
+    copies.start(("sum", 1), outbox.at[1], inbox.at[1], (cx, peers[1]))
+    hidden = partial_ref[:, columns(tp)] + layer_ref[...].astype(jnp.float32)
+    copies.wait(("sum", 3), inbox.at[2], (cx, peers[1]))
+    outbox[2] = (partial_ref[:, columns(peers[2])] + inbox[2].astype(jnp.float32)).astype(
+        jnp.bfloat16
+    )
+    copies.start(("sum", 2), outbox.at[2], inbox.at[3], (cx, peers[2]))
+    copies.wait(("sum", 1), inbox.at[1], (cx, peers[1]))
+    hidden = hidden + inbox[1].astype(jnp.float32)
+    copies.wait(("sum", 2), inbox.at[3], (cx, peers[2]))
+    hidden = hidden + inbox[3].astype(jnp.float32)
+    hidden_ref[...] = hidden
+    squares[0] = lax.dot_general(
+        jnp.ones((8, share), jnp.float32),
+        hidden * hidden,
+        (((1,), (1,)), ((), ())),
+        precision=highest_precision,
+        preferred_element_type=jnp.float32,
+    )
+    for j in (3, 2, 1):
+        copies.start(("squares", j), squares.at[0], squares.at[j], (cx, peers[j]))
+    total = squares[0]
+    for j in (1, 2, 3):
+        copies.wait(("squares", j), squares.at[j], (cx, peers[j]))
+        total = total + squares[j]
+    scale = lax.rsqrt(total / (share * PIECES) + epsilon)
+    scale = jnp.transpose(jnp.broadcast_to(scale[0:1, :], (rows, rows)))[:, 0:1]
+    first_row = pl.multiple_of(cx * rows, rows)
+    all_ref[pl.ds(first_row, rows), columns(tp)] = (
+        hidden_ref[...] * scale * gain_ref[:, columns(tp)]
+    ).astype(jnp.bfloat16)
+
+    def place(owner, piece, start, count):
+        return all_ref.at[
+            pl.ds(pl.multiple_of(owner * rows + start, 16), count), columns(piece)
+        ]
+
+    stage, forward, corner, finish = plane_gather(copies, place, rows, half)
+    mine = place(cx, tp, 0, rows)
+    for j in (2, 1):
+        copies.start(("z", j), mine, mine, (cx, peers[j]))
+    stage(0, peers[0])
+
+    def take(j):
+        landed = place(cx, peers[j], 0, rows)
+        copies.wait(("z", j), landed, (cx, peers[j]))
+        if j == 2:
+            copies.start(("z", 3), landed, landed, (cx, peers[1]))
+        stage(j, peers[j])
+
+    expert = (cx // 2).astype(jnp.float32)
+    expert_count = router_ref.shape[1]
+
+    def choice(owner):
+        first, second = [
+            jnp.transpose(jnp.broadcast_to(ids_ref[owner, k : k + 1, :], (rows, rows)))[
+                :, :expert_count
+            ]
+            for k in range(2)
+        ]
+        lanes = lax.broadcasted_iota(jnp.int32, (rows, expert_count), 1).astype(jnp.float32)
+
+        def equal(a, b):
+            return jnp.where(a == b, 1.0, 0.0)
+
+        return (equal(first, lanes) - equal(second, lanes)) * (
+            equal(first, expert) - equal(second, expert)
+        )
+
+    def compute(owner):
+        start = pl.multiple_of(owner // 2 * (2 * rows), 2 * rows)
+        here = pl.ds(start, 2 * rows)
+        logits = jnp.dot(all_ref[here], router_ref[...], preferred_element_type=jnp.float32)
+        select = jnp.concatenate([choice(start // rows), choice(start // rows + 1)])
+        weight = jax.nn.sigmoid(jnp.sum(logits * select, axis=1, keepdims=True))
+        weight = weight * (0.5 * jnp.sum(select * select, axis=1, keepdims=True))
+
+        def lift(n, carry):
+            units = pl.ds(pl.multiple_of(n * 256, 256), 256)
+            gated = jnp.dot(
+                all_ref[here], gate_ref[:, units], preferred_element_type=jnp.float32
+            )
+            lifted = jnp.dot(all_ref[here], up_ref[:, units], preferred_element_type=jnp.float32)
+            activated[:, units] = (gated * jax.nn.sigmoid(gated) * lifted).astype(jnp.bfloat16)
+            return carry
+
+        lax.fori_loop(0, hidden_units // 256, lift, 0)
+
+        def lower(n, carry):
+            span = pl.ds(pl.multiple_of(n * 512, 512), 512)
+            product = jnp.dot(
+                activated[...], down_ref[:, span], preferred_element_type=jnp.float32
+            )
+            produced_ref[here, span] = (product * weight).astype(jnp.bfloat16)
+            return carry
+
+        lax.fori_loop(0, width // 512, lower, 0)
+
+    homes = (across, along_x, along_y, cx)
+    order = (3, 2, 1, 0)
+
+    def part(owner, j):
+        return produced_ref.at[
+            pl.ds(pl.multiple_of(owner * rows, rows), rows), columns(peers[j])
+        ]
+
+    def trade(k):
+        other = homes[k] + 1 - 2 * (homes[k] % 2)
+        for j in order:
+            copies.start(("pair", j, k), part(other, j), paired.at[j, k], to_sibling)
+
+    def both(j, k):
+        copies.wait(("pair", j, k), paired.at[j, k], to_sibling)
+        return part(homes[k], j)[...].astype(jnp.float32) + paired[j, k].astype(jnp.float32)
+
+    def send_x(j):
+        x_out[j] = both(j, 1).astype(jnp.bfloat16)
+        copies.start(("x0", j), x_out.at[j, top], x_in.at[j, top], to_x)
+
+    def send_y(j):
+        y_out[j] = both(j, 2).astype(jnp.bfloat16)
+        copies.start(("y1", j), y_out.at[j, low], y_in.at[j, low], to_y)
+
+    def send_corner(j):
+        corner_out[j] = both(j, 0).astype(jnp.bfloat16)
+        copies.start(("cx", j), corner_out.at[j, top], corner_x.at[j], to_x)
+        copies.start(("cy", j), corner_out.at[j, low], corner_y.at[j], to_y)
+
+    def second(j):
+        copies.wait(("cx", j), corner_x.at[j], to_x)
+        y_out[j, top] = (
+            y_out[j, top].astype(jnp.float32) + corner_x[j].astype(jnp.float32)
+        ).astype(jnp.bfloat16)
+        copies.start(("y0", j), y_out.at[j, top], y_in.at[j, top], to_y)
+        copies.wait(("cy", j), corner_y.at[j], to_y)
+        x_out[j, low] = (
+            x_out[j, low].astype(jnp.float32) + corner_y[j].astype(jnp.float32)
+        ).astype(jnp.bfloat16)
+        copies.start(("x1", j), x_out.at[j, low], x_in.at[j, low], to_x)
+
+    def third(j):
+        total = both(j, 3)
+        copies.wait(("x0", j), x_in.at[j, top], to_x)
+        copies.wait(("y1", j), y_in.at[j, low], to_y)
+        copies.wait(("y0", j), y_in.at[j, top], to_y)
+        copies.wait(("x1", j), x_in.at[j, low], to_x)
+        total = total + x_in[j].astype(jnp.float32) + y_in[j].astype(jnp.float32)
+        if j == 2:
+            copies.wait(("z_out", 3), z_in.at[2], (cx, peers[1]))
+            total = total + z_in[2].astype(jnp.float32)
+        if j:
+            slot, peer = {3: (2, 1), 2: (3, 2), 1: (1, 1)}[j]
+            z_out[j] = total.astype(jnp.bfloat16)
+            copies.start(("z_out", j), z_out.at[j], z_in.at[slot], (cx, peers[peer]))
+        return total
+
+    take(1)
+    forward(0, peers[0])
+    take(2)
+    forward(1, peers[1])
+    corner(0, peers[0])
+    take(3)
+    forward(2, peers[2])
+    corner(1, peers[1])
+    for load in loads:
+        load.wait()
+    for j in range(PIECES):
+        finish(j, peers[j], 0)
+    compute(cx)
+    trade(3)
+    forward(3, peers[3])
+    corner(2, peers[2])
+    for j in range(PIECES):
+        finish(j, peers[j], 1)
+    compute(along_x)
+    trade(1)
+    corner(3, peers[3])
+    compute(along_y)
+    trade(2)
+    for j in order:
+        send_x(j)
+    for j in range(PIECES):
+        finish(j, peers[j], 2)
+    compute(across)
+    trade(0)
+    for j in order:
+        send_y(j)
+    for j in order:
+        send_corner(j)
+    second(3)
+    second(2)
+    third(3)
+    second(1)
+    second(0)
+    third(2)
+    third(1)
+    total = third(0) + hidden_ref[...]
+    copies.wait(("z_out", 1), z_in.at[1], (cx, peers[1]))
+    copies.wait(("z_out", 2), z_in.at[3], (cx, peers[2]))
+    total = total + z_in[1].astype(jnp.float32) + z_in[3].astype(jnp.float32)
+    out_ref[...] = total.astype(jnp.bfloat16)
+    copies.drain()
+
+
+def experts_layer(partial_rows, layer_input, gain, router, ids, w_gate, w_up, w_down):
+    rows, share = layer_input.shape
+    width, units = w_gate.shape
+    everyone = 2 * CHIPS * rows
+    in_vmem = pl.BlockSpec(memory_space=pltpu.VMEM)
+    anywhere = pl.BlockSpec(memory_space=pl.ANY)
+    piece = pltpu.VMEM((PIECES, rows, share), jnp.bfloat16)
+    half = pltpu.VMEM((PIECES, rows // 2, share), jnp.bfloat16)
+    work = everyone * 6 * width * units
+    return pl.pallas_call(
+        layer_kernel,
+        out_shape=jax.ShapeDtypeStruct((rows, share), jnp.bfloat16),
+        in_specs=[in_vmem] * 5 + [anywhere] * 3,
+        out_specs=in_vmem,
+        scratch_shapes=[
+            pltpu.VMEM((rows, share), jnp.float32),
+            pltpu.VMEM((everyone, width), jnp.bfloat16),
+            pltpu.VMEM((PIECES, 8, rows), jnp.float32),
+            pltpu.VMEM((width, units), jnp.bfloat16),
+            pltpu.VMEM((width, units), jnp.bfloat16),
+            pltpu.VMEM((units, width), jnp.bfloat16),
+            pltpu.VMEM((2 * rows, units), jnp.bfloat16),
+            pltpu.VMEM((everyone, width), jnp.bfloat16),
+            pltpu.VMEM((PIECES, CHIPS, rows, share), jnp.bfloat16),
+        ]
+        + [piece] * 5
+        + [half] * 2
+        + [piece] * 4
+        + [pltpu.SemaphoreType.DMA((88,)), pltpu.SemaphoreType.DMA((88,))]
+        + [pltpu.SemaphoreType.DMA((3,))],
+        compiler_params=pltpu.CompilerParams(
+            collective_id=2, has_side_effects=True, vmem_limit_bytes=VMEM_BYTES
+        ),
+        cost_estimate=pl.CostEstimate(
+            flops=work, bytes_accessed=6 * width * units, transcendentals=0
+        ),
+        name="experts_layer",
+    )(partial_rows, layer_input, gain, router, ids, w_gate, w_up, w_down)
+
+
+def shards_dense(
+    layer_input,
+    queries,
+    keys,
+    values,
+    gate_input,
+    log_decay,
+    prior_state,
+    attn_gain,
+    out_weight,
+    moe_gain,
+    router,
+    expert_ids,
+    w_gate,
+    w_up,
+    w_down,
+):
+    positions = queries.shape[0]
+    heads_here = log_decay.shape[0]
+    head_size = prior_state.shape[1]
+    me = lax.axis_index("cx")
+    query_vectors = queries.reshape(positions, heads_here, head_size)
+    key_rows = keys.reshape(positions, heads_here, head_size)
+    value_single_float = values.reshape(positions, heads_here, head_size).astype(jnp.float32)
+    running_state = jnp.cumsum(log_decay, axis=1)
+    trailing_rows = jnp.exp(running_state[:, -1:] - running_state)
+    key_single_float = key_rows.astype(jnp.float32) * trailing_rows.T[:, :, None]
+    within_block_state = jnp.einsum(
+        "gpc,gpw->pcw", key_single_float, value_single_float, precision=highest_precision
+    )
+    total_decay = running_state[:, -1]
+    coarse = lax.reduce_precision(total_decay, 8, 7)
+    decay_row = jnp.concatenate(
+        [coarse, total_decay - coarse, jnp.zeros((head_size - 2 * heads_here,), jnp.float32)]
+    )
+    extra = jnp.concatenate(
+        [
+            expert_ids.T.astype(jnp.float32),
+            decay_row[None, :],
+            jnp.zeros((13, head_size), jnp.float32),
+        ]
+    )
+    state_rows = heads_here * head_size
+    block = jnp.concatenate(
+        [within_block_state.reshape(state_rows, head_size), extra]
+    ).astype(jnp.bfloat16)
+    gathered, all_ids = gather_states(block)
+    decays = all_ids[:, 2, :]
+    decays = decays[:, :heads_here] + decays[:, heads_here : 2 * heads_here]
+    peers = decays.shape[0]
+    spot = jnp.arange(peers)
+    earlier = spot < me
+    decays = jnp.where(earlier[:, None], decays, 0.0)
+    later = spot[None, :] > spot[:, None]
+    factor = jnp.exp(jnp.sum(jnp.where(later[:, :, None], decays[None], 0.0), axis=1))
+    factor = jnp.where(earlier[:, None], factor, 0.0)
+    all_states = gathered[:, :state_rows, :].reshape(peers, heads_here, head_size, head_size)
+    incoming_state = jnp.exp(jnp.sum(decays, axis=0))[:, None, None] * prior_state + jnp.sum(
+        factor[:, :, None, None] * all_states.astype(jnp.float32), axis=0
+    )
+    causal = (jnp.arange(positions)[:, None] >= jnp.arange(positions)[None, :])[None]
+    spread = running_state[:, :, None] - running_state[:, None, :]
+    weights = jnp.where(causal, jnp.exp(jnp.where(causal, spread, 0.0)), 0.0)
+    scores = (
+        jnp.einsum("thk,shk->hts", query_vectors, key_rows, preferred_element_type=jnp.float32)
+        * weights
+    )
+    inner = jnp.einsum("hts,shv->thv", scores, value_single_float, precision=highest_precision)
+    carried_contribution = jnp.exp(running_state).T[:, :, None] * jnp.einsum(
+        "rxg,xgd->rxd",
+        query_vectors.astype(jnp.float32),
+        incoming_state,
+        precision=highest_precision,
+    )
+    attended = inner + carried_contribution
+    squares = jnp.mean(attended * attended, axis=-1, keepdims=True)
+    gating = jax.nn.sigmoid(
+        gate_input.astype(jnp.float32).reshape(positions, heads_here, head_size)
+    )
+    normed = (
+        attended * lax.rsqrt(squares + epsilon) * attn_gain.reshape(heads_here, head_size) * gating
+    )
+    normed = normed.astype(jnp.bfloat16).reshape(positions, heads_here * head_size)
+    partial_rows = jnp.dot(normed, out_weight, preferred_element_type=jnp.float32)
+    return experts_layer(
+        partial_rows, layer_input, moe_gain[None, :], router, all_ids, w_gate[0], w_up[0], w_down[0]
+    )
+
+
 def solution(mesh):
     placed = (
         P("cx", "tp"),
@@ -177,6 +720,8 @@
         P("cx", None, "tp"),
         P("cx", "tp", None),
     )
+    dense = mesh.shape["cx"] == 2 * CHIPS and mesh.shape["tp"] == PIECES
+    shards = shards_dense if dense else shards_routed
     return jax.shard_map(
         shards, mesh=mesh, in_specs=placed, out_specs=P("cx", "tp"), check_vma=False
     )

time: 349 us -> 140 us (0.40)
  waiting for transfers between devices: 178 us -> 0 us
  Pallas kernels: 0 us -> 123 us
  blocking collectives: 90.6 us -> 0 us
  matrix products: 31.2 us -> 6.84 us
  other arithmetic: 22.4 us -> 3.88 us
  between operations: 14.2 us -> 0.25 us
  starting transfers between devices: 5.18 us -> 0 us
    pallas_call x0 -> x2, Pallas kernels: none -> 123 us  [the longest x1 107 us: experts_layer(): pl.pallas_call(layer_kernel, out_shape=jax.ShapeDtypeStruct((rows, share)...]
    all_to_all x1 -> x0, blocking collectives: 75.3 us -> none  [shards(): lax.all_to_all(outgoing, 'cx', split_axis=0, concat_axis=0, tiled=True)]
    all_to_all x1 -> x0, waiting for transfers between devices: 70.6 us -> none  [shards(): lax.all_to_all(produced.reshape(owners, slots, columns).astype(jnp.bfloat...]
    psum x1 -> x0, waiting for transfers between devices: 66.5 us -> none  [shards(): hidden_state = lax.psum(partial_rows, 'tp')]
    dot_general x11 -> x5, matrix products: 31.2 us -> 6.84 us  [the longest x1 3.87 us: shards_dense(): jnp.dot(normed, out_weight, preferred_element_type=jnp.float32)]
    reduce_scatter x1 -> x0, waiting for transfers between devices: 20.7 us -> none  [shards(): lax.psum_scatter(moe_rows.astype(jnp.bfloat16), 'tp', scatter_dimension=1...]
    all_gather x1 -> x0, waiting for transfers between devices: 20.4 us -> none  [prefix(): everything = jax.tree.map(lambda part: lax.all_gather(part, axis), shard)]
    unnamed x1 -> x0, blocking collectives: 15.3 us -> none
  transfers between devices with their start and end apart: 4 -> 0, of which waited for: 4 -> 0; matrix products, arithmetic and copies ran while one was open for 2% -> 0% of each run, Pallas kernels for 0% -> 0%
where the time goes in v1:
time: 140 us; the launch traced here: 139 us
  Pallas kernels  123 us (88%)
  matrix products  6.84 us (5%)
  local copies, waits for them, and re-layouts  5.39 us (4%)
  other arithmetic  3.88 us (3%)
    pallas_call x1, Pallas kernels, experts_layer(): pl.pallas_call(layer_kernel, out_shape=jax.ShapeDtypeStruct((rows, share)...  107 us
    pallas_call x1, Pallas kernels, gather_states(): pl.pallas_call(functools.partial(state_kernel, rows, rows // 32 * 16), ou...  16 us
    dot_general x1, matrix products, shards_dense(): jnp.dot(normed, out_weight, preferred_element_type=jnp.float32)  3.87 us
    unnamed x20, local copies, waits for them, and re-layouts  3.47 us

profile of v1, /device:TPU:0, one launch (start us, length us, event | category | flops | bytes accessed | tf_op | source)
XLA Modules:
  0.0 139.2 jit_solution(16164635329082724906)
XLA Ops:
  0.0 0.0 copy-start
  0.0 0.0 copy-start.4
  0.0 1.0 reduce_window_sum.11
  1.0 0.2 slice_reduce_fusion
  1.2 0.1 maximum_bitcast_fusion
  1.3 0.1 exponential_bitcast_fusion.1
  1.4 1.1 copy.43
  2.5 0.0 copy-done
  2.5 0.4 convolution_convert_fusion
  3.0 0.7 fusion.17
  3.6 0.2 concatenate.9.block_ref
  3.9 16.0 %gather_states.1 = (bf16[8,1040,128]{2,1,0:T(8,128)(2,1)S(1)}, f32[8,16,128]{2,1,0:T(8,128)S(1)}) custom-call(bf16[1040,128]{1,0:T(8,128)(2,1)S(1)} %concatenate.9.block_ref), custom_call_target="tpu_custom_call" | custom-call | tf_op jit(solution)/shard_map/gather_states/pallas_call | solution.py:292
  19.9 0.0 copy-start.5
  20.0 0.1 fusion.18
  20.1 0.1 select_reduce_fusion
  20.2 0.1 exponential_select_fusion
  20.2 0.1 copy.37
  20.3 0.0 copy-start.6
  20.3 0.1 broadcast_bitcast_fusion
  20.4 0.0 copy-start.8
  20.4 1.4 multiply_reduce_fusion
  21.8 0.0 copy-done.4
  21.8 1.6 %fusion.1 = f32[128,8,128]{0,2,1:T(8,128)S(1)} fusion(f32[8,128,128]{2,1,0:T(8,128)S(1)} %bitcast.62, f32[8,128,128]{2,1,0:T(8,128)S(1)} %copy-done.4, f32[8]{0:T(128)S(1)} %exp.40, f32[128,8]{0,1:T(8,128)S(1)} %get-tuple-element.11, bf16[128,1024]{1,0:T(8,128)(2,1)} %param.16), kind=kOutput, calls=%fused_computation.5 | convolution fusion | flops 201719808 | bytes 1839136 | tf_op jit(solution)/shard_map/rxg,xgd->rxd/dot_general | solution.py:684
  23.4 0.0 copy-done.6
  23.4 0.2 convolution_multiply_fusion
  23.7 0.7 multiply_reduce_fusion.1
  24.4 0.0 copy-done.5
  24.4 0.1 add_divide_fusion
  24.6 0.2 copy.40
  24.8 0.0 copy-done.8
  24.8 0.2 multiply_convert_fusion
  25.0 0.0 copy-start.7
  25.0 0.0 copy-start.2
  25.0 0.0 copy-start.3
  25.0 3.9 %fusion.19.partial_ref = f32[128,3072]{1,0:T(8,128)S(1)} fusion(bf16[128,1024]{0,1:T(8,128)(2,1)S(1)} %bitcast.63, bf16[1024,3072]{1,0:T(8,128)(2,1)} %param.23), kind=kOutput, calls=%fused_computation.42 | convolution fusion | flops 805306368 | bytes 8126464 | tf_op jit(solution)/shard_map/dot_general | solution.py:699
  28.9 0.0 copy-done.7
  28.9 0.4 copy.41.router_ref
  29.3 0.0 copy-done.2
  29.3 0.0 copy-done.3
  29.4 0.0 copy-start.1
  29.4 2.3 %copy-done.1 = bf16[1,3072,768]{2,1,0:T(8,128)(2,1)S(1)} copy-done((bf16[1,3072,768]{2,1,0:T(8,128)(2,1)S(1)}, bf16[1,3072,768]{2,1,0:T(8,128)(2,1)}, u32[]{:S(2)}) %copy-start.1) | copy-done | bytes 4718616
  31.7 106.8 %experts_layer.1 = bf16[128,768]{1,0:T(8,128)(2,1)S(1)} custom-call(f32[128,3072]{1,0:T(8,128)S(1)} %fusion.19.partial_ref, bf16[128,768]{1,0:T(8,128)(2,1)S(1)} %copy-done.2, f32[1,3072]{1,0:T(1,128)S(1)} %bitcast.60, bf16[3072,4]{1,0:T(8,128)(2,1)S(1)} %copy.41.router_ref, f32[8,16,128]{2,1,0:T(8,128)S(1)} %get-tuple-element.7.ids_ref, ...), custom_call_target="tpu_custom_call" | custom-call | flops 14495514624 | bytes 14155776 | tf_op jit(solution)/shard_map/experts_layer/pallas_call | solution.py:585
  138.6 0.7 copy.65
  (9 shorter events, 0.1 us)
Async XLA Ops:
  0.0 2.5 %copy-start = (bf16[128,1024]{1,0:T(8,128)(2,1)S(1)}, bf16[128,1024]{1,0:T(8,128)(2,1)}, u32[]{:S(2)}) copy-start(bf16[128,1024]{1,0:T(8,128)(2,1)} %param.18) | copy-start | bytes 786436
  0.0 21.8 %copy-start.4 = (f32[8,128,128]{2,1,0:T(8,128)S(1)}, f32[8,128,128]{2,1,0:T(8,128)}, u32[]{:S(2)}) copy-start(f32[8,128,128]{2,1,0:T(8,128)} %param.21) | copy-start | bytes 1572868
  19.9 4.5 %copy-start.5 = (bf16[128,1024]{1,0:T(8,128)(2,1)S(1)}, bf16[128,1024]{1,0:T(8,128)(2,1)}, u32[]{:S(2)}) copy-start(bf16[128,1024]{1,0:T(8,128)(2,1)} %param.19) | copy-start | bytes 786436
  20.3 3.1 %copy-start.6 = (bf16[128,1024]{1,0:T(8,128)(2,1)S(1)}, bf16[128,1024]{1,0:T(8,128)(2,1)}, u32[]{:S(2)}) copy-start(bf16[128,1024]{1,0:T(8,128)(2,1)} %param.16) | copy-start | bytes 786436
  20.4 4.4 %copy-start.8 = (f32[1024]{0:T(1024)S(1)}, f32[1024]{0:T(1024)}, u32[]{:S(2)}) copy-start(f32[1024]{0:T(1024)} %param.22) | copy-start | bytes 12292
  25.0 3.9 %copy-start.7 = (bf16[3072,4]{0,1:T(4,128)(2,1)S(1)}, bf16[3072,4]{0,1:T(4,128)(2,1)}, u32[]{:S(2)}) copy-start(bf16[3072,4]{0,1:T(4,128)(2,1)} %param.25) | copy-start | bytes 73732
  25.0 4.3 %copy-start.2 = (bf16[128,768]{1,0:T(8,128)(2,1)S(1)}, bf16[128,768]{1,0:T(8,128)(2,1)}, u32[]{:S(2)}) copy-start(bf16[128,768]{1,0:T(8,128)(2,1)} %layer_ref.1) | copy-start | bytes 589828
  25.0 4.3 %copy-start.3 = (f32[3072]{0:T(1024)S(1)}, f32[3072]{0:T(1024)}, u32[]{:S(2)}) copy-start(f32[3072]{0:T(1024)} %param.24) | copy-start | bytes 36868
  29.4 2.3 %copy-start.1 = (bf16[1,3072,768]{2,1,0:T(8,128)(2,1)S(1)}, bf16[1,3072,768]{2,1,0:T(8,128)(2,1)}, u32[]{:S(2)}) copy-start(bf16[1,3072,768]{2,1,0:T(8,128)(2,1)} %param.27) | copy-start | bytes 14155780

commit v2 on v1

--- a/solution.py
+++ b/solution.py
@@ -164,7 +164,7 @@
 
 
 MESH = pl.DeviceIdType.MESH
-VMEM_BYTES = 46 * 1024 * 1024
+VMEM_BYTES = 50 * 1024 * 1024
 CHIPS = 4
 PIECES = 4
 
@@ -325,6 +325,8 @@
     gate_ref,
     up_ref,
     down_ref,
+    gate_sum,
+    up_sum,
     activated,
     produced_ref,
     paired,
@@ -438,34 +440,45 @@
             equal(first, expert) - equal(second, expert)
         )
 
-    def compute(owner):
-        start = pl.multiple_of(owner // 2 * (2 * rows), 2 * rows)
-        here = pl.ds(start, 2 * rows)
+    def chip_rows(owner):
+        return pl.ds(pl.multiple_of(owner // 2 * (2 * rows), 2 * rows), 2 * rows)
+
+    def lift(owner, piece=None, slot=0, opening=True, closing=True):
+        here = chip_rows(owner)
+        depth = pl.ds(0, width) if piece is None else columns(piece)
+
+        def step(n, carry):
+            units = pl.ds(pl.multiple_of(n * 256, 256), 256)
+            block = all_ref[here, depth]
+            gated = jnp.dot(block, gate_ref[depth, units], preferred_element_type=jnp.float32)
+            lifted = jnp.dot(block, up_ref[depth, units], preferred_element_type=jnp.float32)
+            if not opening:
+                gated = gated + gate_sum[slot, :, units]
+                lifted = lifted + up_sum[slot, :, units]
+            if closing:
+                activated[:, units] = (gated * jax.nn.sigmoid(gated) * lifted).astype(jnp.bfloat16)
+            else:
+                gate_sum[slot, :, units] = gated
+                up_sum[slot, :, units] = lifted
+            return carry
+
+        lax.fori_loop(0, hidden_units // 256, step, 0)
+
+    def lower(k):
+        owner = homes[k]
+        here = chip_rows(owner)
+        first = owner - owner % 2
         logits = jnp.dot(all_ref[here], router_ref[...], preferred_element_type=jnp.float32)
-        select = jnp.concatenate([choice(start // rows), choice(start // rows + 1)])
+        select = jnp.concatenate([choice(first), choice(first + 1)])
         weight = jax.nn.sigmoid(jnp.sum(logits * select, axis=1, keepdims=True))
         weight = weight * (0.5 * jnp.sum(select * select, axis=1, keepdims=True))
-
-        def lift(n, carry):
-            units = pl.ds(pl.multiple_of(n * 256, 256), 256)
-            gated = jnp.dot(
-                all_ref[here], gate_ref[:, units], preferred_element_type=jnp.float32
+        other = owner + 1 - 2 * (owner % 2)
+        for j in order:
+            product = jnp.dot(
+                activated[...], down_ref[:, columns(peers[j])], preferred_element_type=jnp.float32
             )
-            lifted = jnp.dot(all_ref[here], up_ref[:, units], preferred_element_type=jnp.float32)
-            activated[:, units] = (gated * jax.nn.sigmoid(gated) * lifted).astype(jnp.bfloat16)
-            return carry
-
-        lax.fori_loop(0, hidden_units // 256, lift, 0)
-
-        def lower(n, carry):
-            span = pl.ds(pl.multiple_of(n * 512, 512), 512)
-            product = jnp.dot(
-                activated[...], down_ref[:, span], preferred_element_type=jnp.float32
-            )
-            produced_ref[here, span] = (product * weight).astype(jnp.bfloat16)
-            return carry
-
-        lax.fori_loop(0, width // 512, lower, 0)
+            produced_ref[here, columns(peers[j])] = (product * weight).astype(jnp.bfloat16)
+            copies.start(("pair", j, k), part(other, j), paired.at[j, k], to_sibling)
 
     homes = (across, along_x, along_y, cx)
     order = (3, 2, 1, 0)
@@ -474,11 +487,6 @@
         return produced_ref.at[
             pl.ds(pl.multiple_of(owner * rows, rows), rows), columns(peers[j])
         ]
-
-    def trade(k):
-        other = homes[k] + 1 - 2 * (homes[k] % 2)
-        for j in order:
-            copies.start(("pair", j, k), part(other, j), paired.at[j, k], to_sibling)
 
     def both(j, k):
         copies.wait(("pair", j, k), paired.at[j, k], to_sibling)
@@ -525,41 +533,48 @@
             copies.start(("z_out", j), z_out.at[j], z_in.at[slot], (cx, peers[peer]))
         return total
 
+    def lift_sides(j):
+        finish(j, peers[j], 1)
+        for slot, owner in enumerate((along_x, along_y)):
+            lift(owner, peers[j], slot, opening=j == 0, closing=False)
+
     take(1)
     forward(0, peers[0])
     take(2)
     forward(1, peers[1])
     corner(0, peers[0])
+    for load in loads:
+        load.wait()
+    lift_sides(0)
     take(3)
     forward(2, peers[2])
     corner(1, peers[1])
-    for load in loads:
-        load.wait()
-    for j in range(PIECES):
-        finish(j, peers[j], 0)
-    compute(cx)
-    trade(3)
+    lift_sides(1)
     forward(3, peers[3])
     corner(2, peers[2])
-    for j in range(PIECES):
-        finish(j, peers[j], 1)
-    compute(along_x)
-    trade(1)
+    lift_sides(2)
+    finish(3, peers[3], 1)
+    lift(along_x, peers[3], 0, opening=False)
+    lower(1)
     corner(3, peers[3])
-    compute(along_y)
-    trade(2)
+    lift(along_y, peers[3], 1, opening=False)
+    lower(2)
     for j in order:
         send_x(j)
     for j in range(PIECES):
         finish(j, peers[j], 2)
-    compute(across)
-    trade(0)
+    lift(across)
+    lower(0)
     for j in order:
         send_y(j)
     for j in order:
         send_corner(j)
+    for j in range(PIECES):
+        finish(j, peers[j], 0)
+    lift(cx)
     second(3)
     second(2)
+    lower(3)
     third(3)
     second(1)
     second(0)
@@ -594,6 +609,8 @@
             pltpu.VMEM((width, units), jnp.bfloat16),
             pltpu.VMEM((width, units), jnp.bfloat16),
             pltpu.VMEM((units, width), jnp.bfloat16),
+            pltpu.VMEM((2, 2 * rows, units), jnp.float32),
+            pltpu.VMEM((2, 2 * rows, units), jnp.float32),
             pltpu.VMEM((2 * rows, units), jnp.bfloat16),
             pltpu.VMEM((everyone, width), jnp.bfloat16),
             pltpu.VMEM((PIECES, CHIPS, rows, share), jnp.bfloat16),

time: 140 us -> 135 us (0.964)
  Pallas kernels: 123 us -> 120 us
  local copies, waits for them, and re-layouts: 5.39 us -> 3.05 us
    pallas_call x1, Pallas kernels: 107 us -> 104 us  [experts_layer(): pl.pallas_call(layer_kernel, out_shape=jax.ShapeDtypeStruct((rows, share)...]
    unnamed x20 -> x18, local copies, waits for them, and re-layouts: 3.47 us -> 1.14 us
where the time goes in v2:
time: 135 us; the launch traced here: 134 us
  Pallas kernels  120 us (89%)
  matrix products  6.82 us (5%)
  other arithmetic  3.88 us (3%)
  local copies, waits for them, and re-layouts  3.05 us (2%)
    pallas_call x1, Pallas kernels, experts_layer(): pl.pallas_call(layer_kernel, out_shape=jax.ShapeDtypeStruct((rows, share)...  104 us
    pallas_call x1, Pallas kernels, gather_states(): pl.pallas_call(functools.partial(state_kernel, rows, rows // 32 * 16), ou...  16 us
    dot_general x1, matrix products, shards_dense(): jnp.dot(normed, out_weight, preferred_element_type=jnp.float32)  3.85 us

profile of v2, /device:TPU:0, one launch (start us, length us, event | category | flops | bytes accessed | tf_op | source)
XLA Modules:
  0.0 134.4 jit_solution(17144829886648793784)
XLA Ops:
  0.0 0.0 copy-start
  0.0 0.0 copy-start.3
  0.0 1.0 reduce_window_sum.11
  1.0 0.2 slice_reduce_fusion
  1.2 0.1 maximum_bitcast_fusion
  1.3 0.1 exponential_bitcast_fusion.1
  1.4 1.1 copy.43
  2.5 0.0 copy-done
  2.5 0.4 convolution_convert_fusion
  3.0 0.7 fusion.17
  3.6 0.2 concatenate.9.block_ref
  3.9 16.0 %gather_states.1 = (bf16[8,1040,128]{2,1,0:T(8,128)(2,1)S(1)}, f32[8,16,128]{2,1,0:T(8,128)S(1)}) custom-call(bf16[1040,128]{1,0:T(8,128)(2,1)S(1)} %concatenate.9.block_ref), custom_call_target="tpu_custom_call" | custom-call | tf_op jit(solution)/shard_map/gather_states/pallas_call | solution.py:292
  19.9 0.0 copy-start.4
  20.0 0.1 fusion.18
  20.1 0.1 select_reduce_fusion
  20.2 0.1 exponential_select_fusion
  20.2 0.1 copy.37
  20.3 0.0 copy-start.5
  20.3 0.1 broadcast_bitcast_fusion
  20.4 0.0 copy-start.7
  20.4 1.4 %multiply_reduce_fusion = f32[1024,128]{1,0:T(8,128)S(1)} fusion(bf16[8,1040,128]{2,1,0:T(8,128)(2,1)S(1)} %get-tuple-element.8, f32[8,1024]{1,0:T(8,128)S(1)} %broadcast_bitcast_fusion), kind=kLoop, calls=%fused_computation | loop fusion | flops 3014656 | bytes 2654208 | tf_op jit(solution)/shard_map/reduce_sum | solution.py:690
  21.8 0.0 copy-done.3
  21.8 1.6 %fusion.1 = f32[128,8,128]{0,2,1:T(8,128)S(1)} fusion(f32[8,128,128]{2,1,0:T(8,128)S(1)} %bitcast.61, f32[8,128,128]{2,1,0:T(8,128)S(1)} %copy-done.3, f32[8]{0:T(128)S(1)} %exp.40, f32[128,8]{0,1:T(8,128)S(1)} %get-tuple-element.11, bf16[128,1024]{1,0:T(8,128)(2,1)} %param.16), kind=kOutput, calls=%fused_computation.5 | convolution fusion | flops 201719808 | bytes 1839136 | tf_op jit(solution)/shard_map/rxg,xgd->rxd/dot_general | solution.py:701
  23.4 0.0 copy-done.5
  23.4 0.2 convolution_multiply_fusion
  23.7 0.7 multiply_reduce_fusion.1
  24.4 0.0 copy-done.4
  24.4 0.1 add_divide_fusion
  24.6 0.2 copy.40
  24.8 0.0 copy-done.7
  24.8 0.2 multiply_convert_fusion
  25.0 0.0 copy-start.6
  25.0 0.0 copy-start.1
  25.0 0.0 copy-start.2
  25.0 3.8 %fusion.19.partial_ref = f32[128,3072]{1,0:T(8,128)S(1)} fusion(bf16[128,1024]{0,1:T(8,128)(2,1)S(1)} %bitcast.62, bf16[1024,3072]{1,0:T(8,128)(2,1)} %param.23), kind=kOutput, calls=%fused_computation.42 | convolution fusion | flops 805306368 | bytes 8126464 | tf_op jit(solution)/shard_map/dot_general | solution.py:716
  28.9 0.0 copy-done.6
  28.9 0.4 copy.41.router_ref
  29.3 0.0 copy-done.1
  29.3 0.0 copy-done.2
  29.3 104.4 %experts_layer.1 = bf16[128,768]{1,0:T(8,128)(2,1)S(1)} custom-call(f32[128,3072]{1,0:T(8,128)S(1)} %fusion.19.partial_ref, bf16[128,768]{1,0:T(8,128)(2,1)S(1)} %copy-done.1, f32[1,3072]{1,0:T(1,128)S(1)} %bitcast.59, bf16[3072,4]{1,0:T(8,128)(2,1)S(1)} %copy.41.router_ref, f32[8,16,128]{2,1,0:T(8,128)S(1)} %get-tuple-element.7.ids_ref, ...), custom_call_target="tpu_custom_call" | custom-call | flops 14495514624 | bytes 14155776 | tf_op jit(solution)/shard_map/experts_layer/pallas_call | solution.py:600
  133.7 0.7 copy.65
  (9 shorter events, 0.1 us)
Async XLA Ops:
  0.0 2.5 %copy-start = (bf16[128,1024]{1,0:T(8,128)(2,1)S(1)}, bf16[128,1024]{1,0:T(8,128)(2,1)}, u32[]{:S(2)}) copy-start(bf16[128,1024]{1,0:T(8,128)(2,1)} %param.18) | copy-start | bytes 786436
  0.0 21.8 %copy-start.3 = (f32[8,128,128]{2,1,0:T(8,128)S(1)}, f32[8,128,128]{2,1,0:T(8,128)}, u32[]{:S(2)}) copy-start(f32[8,128,128]{2,1,0:T(8,128)} %param.21) | copy-start | bytes 1572868
  19.9 4.5 %copy-start.4 = (bf16[128,1024]{1,0:T(8,128)(2,1)S(1)}, bf16[128,1024]{1,0:T(8,128)(2,1)}, u32[]{:S(2)}) copy-start(bf16[128,1024]{1,0:T(8,128)(2,1)} %param.19) | copy-start | bytes 786436
  20.3 3.1 %copy-start.5 = (bf16[128,1024]{1,0:T(8,128)(2,1)S(1)}, bf16[128,1024]{1,0:T(8,128)(2,1)}, u32[]{:S(2)}) copy-start(bf16[128,1024]{1,0:T(8,128)(2,1)} %param.16) | copy-start | bytes 786436
  20.4 4.4 %copy-start.7 = (f32[1024]{0:T(1024)S(1)}, f32[1024]{0:T(1024)}, u32[]{:S(2)}) copy-start(f32[1024]{0:T(1024)} %param.22) | copy-start | bytes 12292
  25.0 3.9 %copy-start.6 = (bf16[3072,4]{0,1:T(4,128)(2,1)S(1)}, bf16[3072,4]{0,1:T(4,128)(2,1)}, u32[]{:S(2)}) copy-start(bf16[3072,4]{0,1:T(4,128)(2,1)} %param.25) | copy-start | bytes 73732
  25.0 4.3 %copy-start.1 = (bf16[128,768]{1,0:T(8,128)(2,1)S(1)}, bf16[128,768]{1,0:T(8,128)(2,1)}, u32[]{:S(2)}) copy-start(bf16[128,768]{1,0:T(8,128)(2,1)} %layer_ref.1) | copy-start | bytes 589828
  25.0 4.3 %copy-start.2 = (f32[3072]{0:T(1024)S(1)}, f32[3072]{0:T(1024)}, u32[]{:S(2)}) copy-start(f32[3072]{0:T(1024)} %param.24) | copy-start | bytes 36868

commit v3 on v2

--- a/solution.py
+++ b/solution.py
@@ -550,6 +550,8 @@
     forward(2, peers[2])
     corner(1, peers[1])
     lift_sides(1)
+    finish(0, peers[0], 2)
+    lift(across, peers[0], 2, closing=False)
     forward(3, peers[3])
     corner(2, peers[2])
     lift_sides(2)
@@ -561,12 +563,12 @@
     lower(2)
     for j in order:
         send_x(j)
-    for j in range(PIECES):
-        finish(j, peers[j], 2)
-    lift(across)
-    lower(0)
     for j in order:
         send_y(j)
+    for j in range(1, PIECES):
+        finish(j, peers[j], 2)
+        lift(across, peers[j], 2, opening=False, closing=j == 3)
+    lower(0)
     for j in order:
         send_corner(j)
     for j in range(PIECES):
@@ -609,8 +611,8 @@
             pltpu.VMEM((width, units), jnp.bfloat16),
             pltpu.VMEM((width, units), jnp.bfloat16),
             pltpu.VMEM((units, width), jnp.bfloat16),
-            pltpu.VMEM((2, 2 * rows, units), jnp.float32),
-            pltpu.VMEM((2, 2 * rows, units), jnp.float32),
+            pltpu.VMEM((3, 2 * rows, units), jnp.float32),
+            pltpu.VMEM((3, 2 * rows, units), jnp.float32),
             pltpu.VMEM((2 * rows, units), jnp.bfloat16),
             pltpu.VMEM((everyone, width), jnp.bfloat16),
             pltpu.VMEM((PIECES, CHIPS, rows, share), jnp.bfloat16),

time: 135 us -> 127 us (0.941)
  Pallas kernels: 120 us -> 113 us
    pallas_call x1, Pallas kernels: 104 us -> 96.8 us  [experts_layer(): pl.pallas_call(layer_kernel, out_shape=jax.ShapeDtypeStruct((rows, share)...]
where the time goes in v3:
time: 127 us
  Pallas kernels  113 us (89%)
  matrix products  6.82 us (5%)
  other arithmetic  3.88 us (3%)
  local copies, waits for them, and re-layouts  3.05 us (2%)
    pallas_call x1, Pallas kernels, experts_layer(): pl.pallas_call(layer_kernel, out_shape=jax.ShapeDtypeStruct((rows, share)...  96.8 us
    pallas_call x1, Pallas kernels, gather_states(): pl.pallas_call(functools.partial(state_kernel, rows, rows // 32 * 16), ou...  16 us
    dot_general x1, matrix products, shards_dense(): jnp.dot(normed, out_weight, preferred_element_type=jnp.float32)  3.85 us

profile of v3, /device:TPU:0, one launch (start us, length us, event | category | flops | bytes accessed | tf_op | source)
XLA Modules:
  0.0 126.8 jit_solution(2449016548178954999)
XLA Ops:
  0.0 0.0 copy-start
  0.0 0.0 copy-start.3
  0.0 1.0 reduce_window_sum.11
  1.0 0.2 slice_reduce_fusion
  1.2 0.1 maximum_bitcast_fusion
  1.3 0.1 exponential_bitcast_fusion.1
  1.4 1.1 copy.43
  2.5 0.0 copy-done
  2.5 0.4 convolution_convert_fusion
  3.0 0.7 fusion.17
  3.6 0.2 concatenate.9.block_ref
  3.9 16.0 %gather_states.1 = (bf16[8,1040,128]{2,1,0:T(8,128)(2,1)S(1)}, f32[8,16,128]{2,1,0:T(8,128)S(1)}) custom-call(bf16[1040,128]{1,0:T(8,128)(2,1)S(1)} %concatenate.9.block_ref), custom_call_target="tpu_custom_call" | custom-call | tf_op jit(solution)/shard_map/gather_states/pallas_call | solution.py:292
  19.9 0.0 copy-start.4
  20.0 0.1 fusion.18
  20.1 0.1 select_reduce_fusion
  20.2 0.1 exponential_select_fusion
  20.2 0.1 copy.37
  20.3 0.0 copy-start.5
  20.3 0.1 broadcast_bitcast_fusion
  20.4 0.0 copy-start.7
  20.4 1.4 %multiply_reduce_fusion = f32[1024,128]{1,0:T(8,128)S(1)} fusion(bf16[8,1040,128]{2,1,0:T(8,128)(2,1)S(1)} %get-tuple-element.8, f32[8,1024]{1,0:T(8,128)S(1)} %broadcast_bitcast_fusion), kind=kLoop, calls=%fused_computation | loop fusion | flops 3014656 | bytes 2654208 | tf_op jit(solution)/shard_map/reduce_sum | solution.py:692
  21.8 0.0 copy-done.3
  21.8 1.6 %fusion.1 = f32[128,8,128]{0,2,1:T(8,128)S(1)} fusion(f32[8,128,128]{2,1,0:T(8,128)S(1)} %bitcast.61, f32[8,128,128]{2,1,0:T(8,128)S(1)} %copy-done.3, f32[8]{0:T(128)S(1)} %exp.40, f32[128,8]{0,1:T(8,128)S(1)} %get-tuple-element.11, bf16[128,1024]{1,0:T(8,128)(2,1)} %param.16), kind=kOutput, calls=%fused_computation.5 | convolution fusion | flops 201719808 | bytes 1839136 | tf_op jit(solution)/shard_map/rxg,xgd->rxd/dot_general | solution.py:703
  23.4 0.0 copy-done.5
  23.4 0.2 convolution_multiply_fusion
  23.7 0.7 multiply_reduce_fusion.1
  24.4 0.0 copy-done.4
  24.4 0.1 add_divide_fusion
  24.6 0.2 copy.40
  24.8 0.0 copy-done.7
  24.8 0.2 multiply_convert_fusion
  25.0 0.0 copy-start.6
  25.0 0.0 copy-start.1
  25.0 0.0 copy-start.2
  25.0 3.8 %fusion.19.partial_ref = f32[128,3072]{1,0:T(8,128)S(1)} fusion(bf16[128,1024]{0,1:T(8,128)(2,1)S(1)} %bitcast.62, bf16[1024,3072]{1,0:T(8,128)(2,1)} %param.23), kind=kOutput, calls=%fused_computation.42 | convolution fusion | flops 805306368 | bytes 8126464 | tf_op jit(solution)/shard_map/dot_general | solution.py:718
  28.9 0.0 copy-done.6
  28.9 0.4 copy.41.router_ref
  29.3 0.0 copy-done.1
  29.3 0.0 copy-done.2
  29.3 96.8 %experts_layer.1 = bf16[128,768]{1,0:T(8,128)(2,1)S(1)} custom-call(f32[128,3072]{1,0:T(8,128)S(1)} %fusion.19.partial_ref, bf16[128,768]{1,0:T(8,128)(2,1)S(1)} %copy-done.1, f32[1,3072]{1,0:T(1,128)S(1)} %bitcast.59, bf16[3072,4]{1,0:T(8,128)(2,1)S(1)} %copy.41.router_ref, f32[8,16,128]{2,1,0:T(8,128)S(1)} %get-tuple-element.7.ids_ref, ...), custom_call_target="tpu_custom_call" | custom-call | flops 14495514624 | bytes 14155776 | tf_op jit(solution)/shard_map/experts_layer/pallas_call | solution.py:602
  126.1 0.7 copy.65
  (9 shorter events, 0.1 us)
Async XLA Ops:
  0.0 2.5 %copy-start = (bf16[128,1024]{1,0:T(8,128)(2,1)S(1)}, bf16[128,1024]{1,0:T(8,128)(2,1)}, u32[]{:S(2)}) copy-start(bf16[128,1024]{1,0:T(8,128)(2,1)} %param.18) | copy-start | bytes 786436
  0.0 21.8 %copy-start.3 = (f32[8,128,128]{2,1,0:T(8,128)S(1)}, f32[8,128,128]{2,1,0:T(8,128)}, u32[]{:S(2)}) copy-start(f32[8,128,128]{2,1,0:T(8,128)} %param.21) | copy-start | bytes 1572868
  19.9 4.5 %copy-start.4 = (bf16[128,1024]{1,0:T(8,128)(2,1)S(1)}, bf16[128,1024]{1,0:T(8,128)(2,1)}, u32[]{:S(2)}) copy-start(bf16[128,1024]{1,0:T(8,128)(2,1)} %param.19) | copy-start | bytes 786436
  20.3 3.1 %copy-start.5 = (bf16[128,1024]{1,0:T(8,128)(2,1)S(1)}, bf16[128,1024]{1,0:T(8,128)(2,1)}, u32[]{:S(2)}) copy-start(bf16[128,1024]{1,0:T(8,128)(2,1)} %param.16) | copy-start | bytes 786436
  20.4 4.4 %copy-start.7 = (f32[1024]{0:T(1024)S(1)}, f32[1024]{0:T(1024)}, u32[]{:S(2)}) copy-start(f32[1024]{0:T(1024)} %param.22) | copy-start | bytes 12292
  25.0 3.9 %copy-start.6 = (bf16[3072,4]{0,1:T(4,128)(2,1)S(1)}, bf16[3072,4]{0,1:T(4,128)(2,1)}, u32[]{:S(2)}) copy-start(bf16[3072,4]{0,1:T(4,128)(2,1)} %param.25) | copy-start | bytes 73732
  25.0 4.3 %copy-start.1 = (bf16[128,768]{1,0:T(8,128)(2,1)S(1)}, bf16[128,768]{1,0:T(8,128)(2,1)}, u32[]{:S(2)}) copy-start(bf16[128,768]{1,0:T(8,128)(2,1)} %layer_ref.1) | copy-start | bytes 589828
  25.0 4.3 %copy-start.2 = (f32[3072]{0:T(1024)S(1)}, f32[3072]{0:T(1024)}, u32[]{:S(2)}) copy-start(f32[3072]{0:T(1024)} %param.24) | copy-start | bytes 36868
